TPU v7x, 768 devices: a whole 4x8x12 slice. The times are simulated.
768 devices in a mesh: tile: 96 (over y_hi, z, core), lev: 8 (over x, y_lo).
Axes of the slice: x: 4, y: 8 (y_hi: 4, y_lo: 2; y = y_hi * 2 + y_lo), z: 12, core: 2. Of those that a mesh axis runs over, the one named last changes fastest.
Arguments:
- control: float32 [128, 98304], P('lev', 'tile'), may hold values from -6 to 6
- ensemble: bfloat16 [32, 128, 98304], P(None, 'lev', 'tile'), may hold values from -6 to 6
- obs_owner: int32 [73728, 1], P('tile'), may hold values from 0 to 95; in each aligned block of 768 rows (0 to 767, 768 to 1535, ...) at most 16 rows name the same one
- obs_column: int32 [73728], P('tile'), may hold values from 0 to 1023
- obs_profile: float32 [128, 73728], P('lev', 'tile'), may hold values from -8 to 8
Outputs:
- increment: float32 [128, 98304], P('lev', 'tile')
Inputs may be any that keep to these rules, and one draw needn't show every extreme that they name: `obs_owner`: among the profiles of one tile (aligned blocks of 768 rows), no owner tile is named more than 16 times, a bound that some block reaches.
All inputs are finite; a program needn't handle non-finite values.
Results may differ from a plain program's by a relative error of at most 0.012.
The roundings to bfloat16 on the way count: a program that leaves them out, or rounds other values in their place, can miss the bound.
Values may be sent and summed in bfloat16 or wider, within the bound.
A program may use at most 32 MiB of HBM per device.

v0:
```python
import math

import jax
import jax.numpy as jnp
from jax import lax
from jax.sharding import PartitionSpec as P

VSCALE = 16


def extended(block, sides, width):
    for axis, dim in sides:
        count = lax.axis_size(axis)
        forward = [(i, i + 1) for i in range(count - 1)]
        forward.append((count - 1, 0))
        backward = [(target, source) for source, target in forward]
        low = lax.ppermute(
            lax.slice_in_dim(block, block.shape[dim] - width, None, axis=dim), axis, forward
        )
        high = lax.ppermute(lax.slice_in_dim(block, 0, width, axis=dim), axis, backward)
        block = jnp.concatenate([low, block, high], axis=dim)
    return block


def shards(control, ensemble, obs_owner, obs_column, obs_profile):
    tiles = lax.axis_size("tile")
    groups = lax.axis_size("lev")
    lev_dev, columns = control.shape
    members = ensemble.shape[0]
    obs_dev = obs_profile.shape[1]
    capacity = 2 * obs_dev // tiles
    levels = lev_dev * groups
    owner = obs_owner[:, 0]
    onehot = (owner[:, None] == jnp.arange(tiles)[None, :]).astype(jnp.int32)
    earlier = jnp.cumsum(onehot, axis=0) - onehot
    slot = jnp.sum(earlier * onehot, axis=1)
    position = owner * capacity + slot
    send_profile = (
        jnp.zeros((lev_dev, tiles * capacity), jnp.float32).at[:, position].set(obs_profile)
    )
    send_column = (
        jnp.zeros((1, tiles * capacity), jnp.float32)
        .at[0, position]
        .set(obs_column.astype(jnp.float32))
    )
    got_profile, got_column = (
        lax.all_to_all(send_profile, "tile", split_axis=1, concat_axis=1, tiled=True),
        lax.all_to_all(send_column, "tile", split_axis=1, concat_axis=1, tiled=True),
    )
    field = control.at[:, got_column[0].astype(jnp.int32)].add(got_profile)
    weighted = (ensemble.astype(jnp.float32) * field[None, :, :]).astype(jnp.bfloat16)
    band = columns // 2
    padded = extended(weighted, (("tile", 2),), band)
    flat = padded.reshape(members * lev_dev, columns + 2 * band)
    block = min(512, columns)
    rows_a = jnp.arange(block + 2 * band)[:, None]
    cols_b = jnp.arange(block)[None, :]
    offset = jnp.abs(rows_a - cols_b - band)
    table = jnp.where(
        offset <= band, jnp.exp(-offset.astype(jnp.float32) / band) / math.sqrt(band), 0.0
    ).astype(jnp.bfloat16)
    pieces = []
    for start in range(0, columns, block):
        window = flat[:, start : start + block + 2 * band]
        pieces.append(jnp.dot(window, table, preferred_element_type=jnp.float32))
    smooth = jnp.concatenate(pieces, axis=1).astype(jnp.bfloat16).reshape(members, lev_dev, columns)
    smooth_cols = lax.all_to_all(smooth, "lev", split_axis=2, concat_axis=1, tiled=True)
    levels_i = jnp.arange(levels)
    apart = jnp.abs(levels_i[:, None] - levels_i[None, :]).astype(jnp.float32)
    vert_table = (jnp.exp(-(apart * apart) / (2.0 * VSCALE * VSCALE)) / math.sqrt(VSCALE)).astype(
        jnp.bfloat16
    )
    vertical = jnp.einsum(
        "ij,mjc->mic", vert_table, smooth_cols, preferred_element_type=jnp.float32
    ).astype(jnp.bfloat16)
    returned = lax.all_to_all(vertical, "lev", split_axis=1, concat_axis=2, tiled=True)
    summed = jnp.sum(ensemble.astype(jnp.float32) * returned.astype(jnp.float32), axis=0)
    return summed * (1.0 / (members - 1))


def solution(mesh):
    in_specs = (
        P("lev", "tile"),
        P(None, "lev", "tile"),
        P("tile", None),
        P("tile"),
        P("lev", "tile"),
    )
    out_specs = P("lev", "tile")
    return jax.shard_map(shards, mesh=mesh, in_specs=in_specs, out_specs=out_specs, check_vma=False)
```

profile of v0, /device:TPU:8, one launch (start us, length us, event | category | flops | bytes accessed | tf_op | source)
XLA Modules:
  0.0 156.9 jit_solution(8113887390698482974)
XLA Ops:
  0.0 0.7 convert_element_type.69
  1.5 1.9 %reduce-window.6 = s32[96,6,128]{2,0,1:T(8,128)S(1)} reduce-window(s32[96,6,128]{2,0,1:T(8,128)S(1)} %fusion.19, s32[]{:T(128)} %constant.13.clone.1), window={size=1x1x128 pad=0_0x0_0x127_0}, to_apply=%region_0.0 | reduce-window | flops 9363456 | bytes 589828 | tf_op jit(solution)/shard_map/reduce-window
  4.5 3.4 %scatter_custom_fusion = f32[1536]{0:T(1024)S(1)} fusion(s32[768]{0:T(1024)S(1)} %fusion.27, f32[768]{0:T(1024)S(1)} %convert_element_type.69, f32[]{:T(128)} %constant.11.clone.1), kind=kCustom, calls=%fused_computation.41 | custom fusion | bytes 6148 | tf_op jit(solution)/shard_map/scatter | solution.py:44
  8.6 21.1 %all-to-all-start = ((f32[1,96,16]{2,0,1:T(1,128)}), f32[1,96,16]{2,0,1:T(1,128)S(1)}, u32[]{:S(2)}, u32[]{:S(2)}) async-start(f32[1,96,16]{2,0,1:T(1,128)} %bitcast.1), calls=%async_computation | async-start | bytes 98304 | tf_op jit(solution)/shard_map/all_to_all | solution.py:48
  29.7 1.0 copy.40
  30.8 4.4 %scatter_custom_fusion.1 = f32[16,1536]{0,1:T(8,128)S(1)} fusion(s32[768]{0:T(1024)S(1)} %fusion.27, f32[768,16]{1,0:T(8,128)S(1)} %copy.40, f32[]{:T(128)} %constant.11.clone.1), kind=kCustom, calls=%fused_computation.21 | custom fusion | bytes 98308 | tf_op jit(solution)/shard_map/scatter | solution.py:39
  35.2 0.9 reshape.103
  36.1 8.4 %all-to-all-done = f32[1,96,16]{2,0,1:T(1,128)S(1)} async-done(((f32[1,96,16]{2,0,1:T(1,128)}), f32[1,96,16]{2,0,1:T(1,128)S(1)}, u32[]{:S(2)}, u32[]{:S(2)}) %all-to-all-start) | async-done | bytes 6176 | tf_op jit(solution)/shard_map/all_to_all | solution.py:48
  44.5 7.2 %all-to-all-start.1 = ((f32[96,1,256]{2,1,0:T(1,128)}), f32[96,1,256]{2,1,0:T(1,128)S(1)}, u32[]{:S(2)}, u32[]{:S(2)}) async-start(f32[96,1,256]{2,1,0:T(1,128)} %reshape.103), calls=%async_computation.1 | async-start | bytes 196608 | tf_op jit(solution)/shard_map/all_to_all | solution.py:47
  52.2 15.8 %all-to-all-done.1 = f32[96,1,256]{2,1,0:T(1,128)S(1)} async-done(((f32[96,1,256]{2,1,0:T(1,128)}), f32[96,1,256]{2,1,0:T(1,128)S(1)}, u32[]{:S(2)}, u32[]{:S(2)}) %all-to-all-start.1) | async-done | bytes 98336 | tf_op jit(solution)/shard_map/all_to_all | solution.py:47
  68.6 0.9 reduce.12
  69.8 9.1 %scatter_fusion = f32[16,1024]{0,1:T(8,128)S(1)} fusion(f32[16,1024]{0,1:T(8,128)S(1)} %copy.41, s32[1536]{0:T(1024)S(1)} %fusion.24, f32[1536,16]{1,0:T(8,128)S(1)} %bitcast.62), kind=kCustom, calls=%fused_computation.2 | custom fusion | flops 24576 | bytes 301056 | tf_op jit(solution)/shard_map/scatter-add | solution.py:50
  79.4 1.9 %collective-permute-start = (bf16[32,16,512]{2,1,0:T(8,128)(2,1)S(1)}, bf16[32,16,512]{2,1,0:T(8,128)(2,1)S(1)}, u32[]{:S(2)}, u32[]{:S(2)}) collective-permute-start(bf16[32,16,512]{2,1,0:T(8,128)(2,1)S(1)} %get-tuple-element.5), channel_id=1, source_target_pairs={{0,8},{8,16},{16,24},{24,32},{32,40},{40,48},{48,56},{56,64},{64,7... | collective-permute-start | bytes 1572872 | tf_op jit(solution)/shard_map/ppermute | solution.py:17
  81.3 8.0 %collective-permute-start.1 = (bf16[32,16,512]{2,1,0:T(8,128)(2,1)S(1)}, bf16[32,16,512]{2,1,0:T(8,128)(2,1)S(1)}, u32[]{:S(2)}, u32[]{:S(2)}) collective-permute-start(bf16[32,16,512]{2,1,0:T(8,128)(2,1)S(1)} %get-tuple-element.6), channel_id=1, source_target_pairs={{8,0},{16,8},{24,16},{32,24},{40,32},{48,40},{56,48},{64,56},{72,6... | collective-permute-start | bytes 1572872 | tf_op jit(solution)/shard_map/ppermute | solution.py:20
  89.4 8.9 %collective-permute-done = bf16[32,16,512]{2,1,0:T(8,128)(2,1)S(1)} collective-permute-done((bf16[32,16,512]{2,1,0:T(8,128)(2,1)S(1)}, bf16[32,16,512]{2,1,0:T(8,128)(2,1)S(1)}, u32[]{:S(2)}, u32[]{:S(2)}) %collective-permute-start) | collective-permute-done | bytes 524320 | tf_op jit(solution)/shard_map/ppermute | solution.py:17
  99.1 1.3 fusion.11
  100.4 1.3 fusion.8
  101.9 5.1 %copy.43 = bf16[32,16,1024]{0,1,2:T(8,128)(2,1)} copy(bf16[32,16,1024]{2,1,0:T(8,128)(2,1)S(1)} %pad_maximum_fusion.1) | data formatting | bytes 2097152 | tf_op jit(solution)/shard_map/concatenate | solution.py:66
  107.0 7.0 %reshape.105 = bf16[8,2,32768]{2,1,0:T(2,128)(2,1)S(1)} reshape(bf16[1024,16,32]{2,1,0:T(8,128)(2,1)} %bitcast.55) | data formatting | bytes 2097152
  113.9 15.9 %all_to_all.48 = bf16[8,2,32768]{2,1,0:T(2,128)(2,1)S(1)} all-to-all(bf16[8,2,32768]{2,1,0:T(2,128)(2,1)S(1)} %reshape.105), channel_id=1, replica_groups=mesh['tile'=96,'lev'=8] {'lev'}, dimensions={0} | all-to-all | bytes 2097152 | tf_op jit(solution)/shard_map/all_to_all | solution.py:67
  129.8 4.5 %reshape.106 = bf16[1024,16,32]{2,1,0:T(8,128)(2,1)} reshape(bf16[8,2,32768]{2,1,0:T(2,128)(2,1)S(1)} %all_to_all.48) | data formatting | bytes 2097152
  134.4 5.6 %copy.45 = bf16[32,8,16,128]{3,2,1,0:T(8,128)(2,1)S(1)} copy(bf16[32,8,16,128]{0,2,3,1:T(8,128)(2,1)} %bitcast.56) | data formatting | bytes 2097152 | tf_op jit(solution)/shard_map/all_to_all | solution.py:67
  140.5 1.0 copy.47
  141.5 14.0 %all_to_all.49 = bf16[32,128,128]{2,0,1:T(8,128)(2,1)S(1)} all-to-all(bf16[32,128,128]{2,0,1:T(8,128)(2,1)S(1)} %copy.47), channel_id=1, replica_groups=mesh['tile'=96,'lev'=8] {'lev'}, dimensions={1} | all-to-all | bytes 2097152 | tf_op jit(solution)/shard_map/all_to_all | solution.py:76
  (27 shorter events, 7.2 us)
Async XLA Ops:
  0.0 51.8 %copy-start.1 = (f32[16,1024]{1,0:T(8,128)S(1)}, f32[16,1024]{1,0:T(8,128)}, u32[]{:S(2)}) copy-start(f32[16,1024]{1,0:T(8,128)} %param.5) | copy-start | bytes 196612
  8.6 35.9 %all-to-all-start = ((f32[1,96,16]{2,0,1:T(1,128)}), f32[1,96,16]{2,0,1:T(1,128)S(1)}, u32[]{:S(2)}, u32[]{:S(2)}) async-start(f32[1,96,16]{2,0,1:T(1,128)} %bitcast.1), calls=%async_computation | async-start | bytes 98304 | tf_op jit(solution)/shard_map/all_to_all | solution.py:48
  29.7 49.3 %copy-start = (bf16[32,16,1024]{2,1,0:T(8,128)(2,1)S(1)}, bf16[32,16,1024]{2,1,0:T(8,128)(2,1)}, u32[]{:S(2)}) copy-start(bf16[32,16,1024]{2,1,0:T(8,128)(2,1)} %param.6) | copy-start | bytes 3145732
  44.5 23.6 %all-to-all-start.1 = ((f32[96,1,256]{2,1,0:T(1,128)}), f32[96,1,256]{2,1,0:T(1,128)S(1)}, u32[]{:S(2)}, u32[]{:S(2)}) async-start(f32[96,1,256]{2,1,0:T(1,128)} %reshape.103), calls=%async_computation.1 | async-start | bytes 196608 | tf_op jit(solution)/shard_map/all_to_all | solution.py:47
  79.4 18.9 %collective-permute-start = (bf16[32,16,512]{2,1,0:T(8,128)(2,1)S(1)}, bf16[32,16,512]{2,1,0:T(8,128)(2,1)S(1)}, u32[]{:S(2)}, u32[]{:S(2)}) collective-permute-start(bf16[32,16,512]{2,1,0:T(8,128)(2,1)S(1)} %get-tuple-element.5), channel_id=1, source_target_pairs={{0,8},{8,16},{16,24},{24,32},{32,40},{40,48},{48,56},{56,64},{64,7... | collective-permute-start | bytes 1572872 | tf_op jit(solution)/shard_map/ppermute | solution.py:17
  81.3 17.6 %collective-permute-start.1 = (bf16[32,16,512]{2,1,0:T(8,128)(2,1)S(1)}, bf16[32,16,512]{2,1,0:T(8,128)(2,1)S(1)}, u32[]{:S(2)}, u32[]{:S(2)}) collective-permute-start(bf16[32,16,512]{2,1,0:T(8,128)(2,1)S(1)} %get-tuple-element.6), channel_id=1, source_target_pairs={{8,0},{16,8},{24,16},{32,24},{40,32},{48,40},{56,48},{64,56},{72,6... | collective-permute-start | bytes 1572872 | tf_op jit(solution)/shard_map/ppermute | solution.py:20
where the time goes:
time: 157 us
  starting transfers between devices  38.3 us (24%)
  local copies, waits for them, and re-layouts  35.7 us (23%)
  waiting for transfers between devices  33.8 us (22%)
  blocking collectives  29.9 us (19%)
  other arithmetic  15.9 us (10%)
  matrix products  3.02 us (2%)
    all_to_all x1, starting transfers between devices, shards(): lax.all_to_all(send_column, 'tile', split_axis=1, concat_axis=1, tiled=True)  21.1 us
    all_to_all x1, blocking collectives, shards(): lax.all_to_all(smooth, 'lev', split_axis=2, concat_axis=1, tiled=True)  15.9 us
    all_to_all x1, waiting for transfers between devices, shards(): lax.all_to_all(send_profile, 'tile', split_axis=1, concat_axis=1, tiled=T...  15.8 us
    all_to_all x1, blocking collectives, shards(): lax.all_to_all(vertical, 'lev', split_axis=1, concat_axis=2, tiled=True)  14 us
    unnamed x10, local copies, waits for them, and re-layouts  13.9 us
    scatter-add x1, other arithmetic, shards(): field = control.at[:, got_column[0].astype(jnp.int32)].add(got_profile)  9.06 us
    ppermute x1, waiting for transfers between devices, extended(): lax.ppermute(lax.slice_in_dim(block, block.shape[dim] - width, None, axis...  8.88 us
    all_to_all x1, waiting for transfers between devices, shards(): lax.all_to_all(send_column, 'tile', split_axis=1, concat_axis=1, tiled=True)  8.42 us
  transfers between devices with their start and end apart: 4, of which 4 were waited for; matrix products, arithmetic and copies ran while one was open for 4% of the time, Pallas kernels for 0%

commit v1 on v0

v1 whole, which is shorter than its diff:
```python
import functools
import math

import jax
import jax.numpy as jnp
from jax import lax
from jax.experimental import pallas as pl
from jax.experimental.pallas import tpu as pltpu
from jax.sharding import PartitionSpec as P

MESH = pl.DeviceIdType.MESH
VSCALE = 16
Y_HI, Z = 4, 12
TILES = Y_HI * Z * 2
LEV = 8
GROUPS = 2 * Y_HI
SLOTS = 16
BAND = 512


def split3(x):
    high = x.astype(jnp.bfloat16)
    rest = x - high.astype(jnp.float32)
    middle = rest.astype(jnp.bfloat16)
    low = (rest - middle.astype(jnp.float32)).astype(jnp.bfloat16)
    return high, middle, low


def bits(mask):
    return jnp.where(mask, 1.0, 0.0).astype(jnp.bfloat16)


def kernel(
    control, ensemble, owner, column, profile, out,
    ens, field, weighted, hor, ver, rank, sorted_, first, second, third, lhs, hot, part, parts,
    local, e_send, e_recv, eh_send, eh_recv, a_send, a_recv, b_send, b_recv,
    f_send, f_recv, fh_send, fh_recv, p_send, p_recv,
):
    tile, lev = lax.axis_index("tile"), lax.axis_index("lev")
    core, z, y_hi = lax.rem(tile, 2), lax.rem(tile // 2, Z), tile // (2 * Z)
    mine = y_hi * 2 + core
    right, left = lax.rem(tile + 1, TILES), lax.rem(tile + TILES - 1, TILES)

    def lev_at(r):
        return lax.rem(lev + r, LEV)

    def group_at(r):
        return lax.rem(mine + r, GROUPS)

    def z_at(r):
        return lax.rem(z + r, Z)

    def tile_of(group, zz):
        return ((group // 2) * Z + zz) * 2 + lax.rem(group, 2)

    def rows(g):
        return pl.ds(pl.multiple_of(g * 16, 16), 16)

    barrier = pltpu.get_barrier_semaphore()
    for r in range(1, GROUPS):
        pl.semaphore_signal(
            barrier, inc=1, device_id={"tile": tile_of(group_at(r), z)}, device_id_type=MESH
        )
    for r in range(1, Z):
        pl.semaphore_signal(
            barrier, inc=1, device_id={"tile": tile_of(mine, z_at(r))}, device_id_type=MESH
        )
    for r in range(1, LEV):
        pl.semaphore_signal(barrier, inc=1, device_id={"lev": lev_at(r)}, device_id_type=MESH)
    for side in (left, right):
        pl.semaphore_signal(barrier, inc=1, device_id={"tile": side}, device_id_type=MESH)

    members = ens.shape[0]
    own = pltpu.make_async_copy(
        ensemble.at[pl.ds(lev * members, members)],
        ens.at[:, rows(lev), pl.ds(BAND, 1024)],
        local,
    )
    own.start()

    row = lax.broadcasted_iota(jnp.int32, (GROUPS * 16, 768), 0)
    named = ((row >> 5) * Z + (row & 15)) * 2 + ((row >> 4) & 1)
    hit = jnp.logical_and(owner[...] == named, (row & 15) < Z)
    hits = bits(hit)
    upper = bits(
        lax.broadcasted_iota(jnp.int32, (256, 256), 0)
        < lax.broadcasted_iota(jnp.int32, (256, 256), 1)
    )
    base = jnp.zeros((GROUPS * 16, 1), jnp.float32)
    for b in range(3):
        lanes = slice(b * 256, b * 256 + 256)
        before = jnp.dot(hits[:, lanes], upper, preferred_element_type=jnp.float32) + base
        rank[:, lanes] = jnp.where(hit[:, lanes], before, -1.0)
        base = base + jnp.sum(hits[:, lanes].astype(jnp.float32), axis=1, keepdims=True)
    high, middle, low = split3(profile[...])
    col = column[...]
    which = lax.broadcasted_iota(jnp.int32, (16, 768), 0)
    cols = jnp.where(which == 0, col & -8, jnp.where(which == 1, col & 7, 0))
    table = jnp.concatenate(
        [high, middle, low, cols.astype(jnp.float32).astype(jnp.bfloat16)]
        + [jnp.zeros((64, 768), jnp.bfloat16)],
        axis=0,
    )
    lane = lax.broadcasted_iota(jnp.int32, (GROUPS * 16, 128), 1)
    for half in range(2):
        packed = jnp.zeros((GROUPS * 16, 128), jnp.float32)
        for s in range(half * 8, half * 8 + 8):
            got = lax.dot_general(
                bits(rank[...] == float(s)),
                table,
                (((1,), (1,)), ((), ())),
                preferred_element_type=jnp.float32,
            )
            total = got + pltpu.roll(got, 112, 1) + pltpu.roll(got, 96, 1)
            at = (s - half * 8) * 16
            total = pltpu.roll(total, at, 1) if at else total
            packed = jnp.where((lane >> 4) == (s - half * 8), total, packed)
            place = pltpu.roll(got + pltpu.roll(got, 127, 1), (s - 48) % 128, 1)
            if s == 0:
                places = jnp.where(lane == 0, place, 0.0)
            else:
                places = jnp.where(lane == s, place, sorted_[:, 256:384])
            sorted_[:, 256:384] = places
        sorted_[:, half * 128 : half * 128 + 128] = packed

    apart = (
        lax.broadcasted_iota(jnp.int32, hor.shape, 0)
        - lax.broadcasted_iota(jnp.int32, hor.shape, 1)
        - BAND
    )
    apart = jnp.abs(apart)
    hor[...] = jnp.where(
        apart <= BAND, jnp.exp(-apart.astype(jnp.float32) / BAND) / math.sqrt(BAND), 0.0
    ).astype(jnp.bfloat16)
    apart = (
        lax.broadcasted_iota(jnp.int32, ver.shape, 0)
        - lax.broadcasted_iota(jnp.int32, ver.shape, 1)
    ).astype(jnp.float32)
    ver[...] = (jnp.exp(-(apart * apart) / (2.0 * VSCALE * VSCALE)) / math.sqrt(VSCALE)).astype(
        jnp.bfloat16
    )
    third[pl.ds(Z, 16 - Z)] = jnp.zeros((16 - Z, 8, 384), jnp.float32)
    own.wait()

    pl.semaphore_wait(barrier, (GROUPS - 1) + (Z - 1) + (LEV - 1) + 2)

    for r in range(1, GROUPS):
        pltpu.make_async_remote_copy(
            src_ref=sorted_.at[rows(group_at(r))],
            dst_ref=first.at[r],
            send_sem=a_send,
            recv_sem=a_recv,
            device_id={"tile": tile_of(group_at(r), z)},
            device_id_type=MESH,
        ).start()

    e_copies = []
    for r in range(1, LEV):
        copy = pltpu.make_async_remote_copy(
            src_ref=ensemble.at[pl.ds(lev_at(r) * members, members)],
            dst_ref=ens.at[:, rows(lev), pl.ds(BAND, 1024)],
            send_sem=e_send.at[r],
            recv_sem=e_recv.at[r],
            device_id={"lev": lev_at(r)},
            device_id_type=MESH,
        )
        copy.start()
        e_copies.append(copy)

    def to_sides(buffer, g, send, recv):
        for side, (target, source, dest) in enumerate(
            ((right, 1024, 0), (left, BAND, BAND + 1024))
        ):
            lead = (slice(None),) if len(buffer.shape) == 3 else ()
            pltpu.make_async_remote_copy(
                src_ref=buffer.at[lead + (rows(g), pl.ds(source, BAND))],
                dst_ref=buffer.at[lead + (rows(g), pl.ds(dest, BAND))],
                send_sem=send,
                recv_sem=recv.at[side],
                device_id={"tile": target},
                device_id_type=MESH,
            ).start()

    def all_sent(ref, sem):
        pltpu.make_async_remote_copy(
            src_ref=ref, dst_ref=ref, send_sem=sem, recv_sem=sem,
            device_id={"tile": right}, device_id_type=MESH,
        ).wait_send()

    def all_here(ref, sem):
        pltpu.make_async_remote_copy(
            src_ref=ref, dst_ref=ref, send_sem=sem, recv_sem=sem,
            device_id={"tile": right}, device_id_type=MESH,
        ).wait_recv()

    first[0] = sorted_[rows(mine)]
    to_sides(ens, lev, eh_send, eh_recv)

    all_here(first.at[pl.ds(1, GROUPS - 1)], a_recv)
    for zz in range(Z):
        second[zz] = first[:, zz, :]
    for r in range(1, Z):
        pltpu.make_async_remote_copy(
            src_ref=second.at[z_at(r)],
            dst_ref=third.at[r],
            send_sem=b_send,
            recv_sem=b_recv,
            device_id={"tile": tile_of(mine, z_at(r))},
            device_id_type=MESH,
        ).start()
    third[0] = second[z]
    all_here(third.at[pl.ds(1, Z - 1)], b_recv)

    where = third[:, :, 256:384].reshape(128, 128)
    cell = lax.broadcasted_iota(jnp.int32, (128, 1024), 1).astype(jnp.float32)
    for half in range(2):
        turned = third[:, :, half * 128 : half * 128 + 128].reshape(128, 128).T
        pieces = split3(turned)
        for k in range(8):
            s = half * 8 + k
            for n, piece in enumerate(pieces):
                lhs[n * 16 : n * 16 + 16, s * 128 : s * 128 + 128] = piece[k * 16 : k * 16 + 16]
            hot[s * 128 : s * 128 + 128, :] = bits(where[:, s : s + 1] == cell)
    added = jnp.dot(lhs[...], hot[...], preferred_element_type=jnp.float32)
    added = added[0:16] + added[16:32] + added[32:48]
    field[rows(lev), pl.ds(BAND, 1024)] = control[...] + added

    f_copies = []
    for r in range(1, LEV):
        copy = pltpu.make_async_remote_copy(
            src_ref=field.at[rows(lev), pl.ds(BAND, 1024)],
            dst_ref=field.at[rows(lev), pl.ds(BAND, 1024)],
            send_sem=f_send.at[r],
            recv_sem=f_recv.at[r],
            device_id={"lev": lev_at(r)},
            device_id_type=MESH,
        )
        copy.start()
        f_copies.append(copy)
    to_sides(field, lev, fh_send, fh_recv)
    for r in range(1, LEV):
        e_copies[r - 1].wait_recv()
        to_sides(ens, lev_at(LEV - r), eh_send, eh_recv)
    for r in range(1, LEV):
        f_copies[r - 1].wait_recv()
        to_sides(field, lev_at(LEV - r), fh_send, fh_recv)
    for side, at in enumerate((0, BAND + 1024)):
        all_here(ens.at[:, :, pl.ds(at, BAND)], eh_recv.at[side])
        all_here(field.at[:, pl.ds(at, BAND)], fh_recv.at[side])

    levels = ens.shape[1]

    def weigh(g, carry):
        here = field[rows(g), :]
        for m in range(members):
            at = pl.ds(pl.multiple_of(m * levels + g * 16, 16), 16)
            weighted[at, :] = (ens[m, rows(g), :].astype(jnp.float32) * here).astype(jnp.bfloat16)
        return carry

    lax.fori_loop(0, LEV, weigh, 0)

    for k in range(4):
        at = k * 256
        smooth = jnp.dot(
            weighted[:, at : at + 256 + 2 * BAND], hor[...], preferred_element_type=jnp.float32
        ).astype(jnp.bfloat16)
        total = jnp.zeros((levels, 256), jnp.float32)
        for m in range(members):
            vertical = jnp.dot(
                ver[...], smooth[m * levels : m * levels + levels],
                preferred_element_type=jnp.float32,
            ).astype(jnp.bfloat16)
            total += ens[m, :, BAND + at : BAND + at + 256].astype(jnp.float32) * vertical.astype(
                jnp.float32
            )
        part[:, at : at + 256] = total.astype(jnp.bfloat16)
        if k % 2 == 1:
            lanes = pl.ds((k - 1) * 256, 512)
            for r in range(1, LEV):
                pltpu.make_async_remote_copy(
                    src_ref=part.at[rows(lev_at(r)), lanes],
                    dst_ref=parts.at[r, :, lanes],
                    send_sem=p_send,
                    recv_sem=p_recv.at[k // 2],
                    device_id={"lev": lev_at(r)},
                    device_id_type=MESH,
                ).start()
    parts[0] = part[rows(lev), :]
    for k in range(2):
        lanes = pl.ds(k * 512, 512)
        all_here(parts.at[pl.ds(1, LEV - 1), :, lanes], p_recv.at[k])
        total = parts[0, :, lanes].astype(jnp.float32)
        for r in range(1, LEV):
            total += parts[r, :, lanes].astype(jnp.float32)
        out[:, lanes] = total * (1.0 / (LEV * members - 1))

    for copy in e_copies + f_copies:
        copy.wait_send()
    all_sent(first.at[pl.ds(1, GROUPS - 1)], a_send)
    all_sent(third.at[pl.ds(1, Z - 1)], b_send)
    all_sent(ens.at[:, :, pl.ds(BAND, 1024)], eh_send)
    all_sent(field.at[:, pl.ds(BAND, 1024)], fh_send)
    all_sent(parts.at[pl.ds(1, LEV - 1)], p_send)


def shards(control, ensemble, obs_owner, obs_column, obs_profile):
    members = ensemble.shape[0] // LEV
    levels = control.shape[0] * LEV
    wide = control.shape[1] + 2 * BAND
    vmem = pl.BlockSpec(memory_space=pltpu.VMEM)
    dma = pltpu.SemaphoreType.DMA
    return pl.pallas_call(
        kernel,
        out_shape=jax.ShapeDtypeStruct(control.shape, jnp.float32),
        in_specs=[vmem, pl.BlockSpec(memory_space=pl.ANY), vmem, vmem, vmem],
        out_specs=vmem,
        scratch_shapes=[
            pltpu.VMEM((members, levels, wide), jnp.bfloat16),
            pltpu.VMEM((levels, wide), jnp.float32),
            pltpu.VMEM((members * levels, wide), jnp.bfloat16),
            pltpu.VMEM((256 + 2 * BAND, 256), jnp.bfloat16),
            pltpu.VMEM((levels, levels), jnp.bfloat16),
            pltpu.VMEM((GROUPS * 16, 768), jnp.float32),
            pltpu.VMEM((GROUPS * 16, 384), jnp.float32),
            pltpu.VMEM((GROUPS, 16, 384), jnp.float32),
            pltpu.VMEM((Z, 8, 384), jnp.float32),
            pltpu.VMEM((16, 8, 384), jnp.float32),
            pltpu.VMEM((48, SLOTS * 128), jnp.bfloat16),
            pltpu.VMEM((SLOTS * 128, control.shape[1]), jnp.bfloat16),
            pltpu.VMEM((levels, control.shape[1]), jnp.bfloat16),
            pltpu.VMEM((LEV,) + control.shape, jnp.bfloat16),
            dma, dma((LEV,)), dma((LEV,)), dma, dma((2,)), dma, dma, dma, dma,
            dma((LEV,)), dma((LEV,)), dma, dma((2,)), dma, dma((2,)),
        ],
        compiler_params=pltpu.CompilerParams(
            collective_id=0, has_side_effects=True, vmem_limit_bytes=60 << 20
        ),
    )(control, ensemble, obs_owner.reshape(1, -1), obs_column.reshape(1, -1), obs_profile)


def solution(mesh):
    in_specs = (
        P("lev", "tile"),
        P(None, "lev", "tile"),
        P("tile", None),
        P("tile"),
        P("lev", "tile"),
    )
    out_specs = P("lev", "tile")
    return jax.shard_map(shards, mesh=mesh, in_specs=in_specs, out_specs=out_specs, check_vma=False)
```

time: 157 us -> 73.5 us (0.47)
  the two profiles are of different devices: /device:TPU:8 before, /device:TPU:1 now
where the time goes in v1:
time: 73.5 us; the launch traced here: 72.9 us
  Pallas kernels  70.1 us (95%)
  local copies, waits for them, and re-layouts  2.74 us (4%)
    pallas_call x1, Pallas kernels, shards(): pl.pallas_call(kernel, out_shape=jax.ShapeDtypeStruct(control.shape, jnp....  70.1 us
    unnamed x1, local copies, waits for them, and re-layouts  1.47 us

profile of v1, /device:TPU:1, one launch (start us, length us, event | category | flops | bytes accessed | tf_op | source)
XLA Modules:
  0.0 72.9 jit_solution(8424226508051488421)
XLA Ops:
  0.0 1.3 %reshape.7.column = s32[1,768]{1,0:T(1,128)} reshape(s32[768]{0:T(1024)} %param.8) | data formatting | bytes 6144 | tf_op jit(solution)/shard_map/reshape | solution.py:338
  1.3 70.1 %shard_map.55 = f32[16,1024]{1,0:T(8,128)} custom-call(f32[16,1024]{1,0:T(8,128)} %control.1, bf16[32,16,1024]{2,1,0:T(8,128)(2,1)} %ensemble.1, s32[1,768]{1,0:T(1,128)} %bitcast.1, s32[1,768]{1,0:T(1,128)} %reshape.7.column, f32[16,768]{1,0:T(8,128)} %profile.1), custom_call_target="tpu_custom_call" | custom-call | tf_op jit(solution)/shard_map/pallas_call | solution.py:312
  71.4 1.5 %copy.7 = f32[16,1024]{1,0:T(8,128)} copy(f32[16,1024]{1,0:T(8,128)} %shard_map.55) | data formatting | bytes 131072

commit v2 on v0

v2 whole, which is shorter than its diff:
```python
import functools
import math

import jax
import jax.numpy as jnp
from jax import lax
from jax.experimental import pallas as pl
from jax.experimental.pallas import tpu as pltpu
from jax.sharding import PartitionSpec as P

MESH = pl.DeviceIdType.MESH
VSCALE = 16
Y_HI, Z = 4, 12
TILES = Y_HI * Z * 2
LEV = 8
GROUPS = 2 * Y_HI
SLOTS = 16
BAND = 512
EARLY = 9
CHUNKS = ((0, 8), (8, 8), (16, 8), (24, 8))


def split3(x):
    high = x.astype(jnp.bfloat16)
    rest = x - high.astype(jnp.float32)
    middle = rest.astype(jnp.bfloat16)
    low = (rest - middle.astype(jnp.float32)).astype(jnp.bfloat16)
    return high, middle, low


def bits(mask):
    return jnp.where(mask, 1.0, 0.0).astype(jnp.bfloat16)


def kernel(
    control, ensemble, owner, column, profile, out,
    ens, field, weighted, hor, ver, rank, sorted_, first, second, third, lhs, hot,
    smooth, gathered, other, total, back,
    local, a_send, a_recv, b_send, b_recv, e_send, e_recv, eh_send, eh_recv,
    fh_send, fh_recv, s_send, s_recv, t_send, t_recv, up, ready,
):
    tile, lev = lax.axis_index("tile"), lax.axis_index("lev")
    core, z, y_hi = lax.rem(tile, 2), lax.rem(tile // 2, Z), tile // (2 * Z)
    mine = y_hi * 2 + core
    right, left = lax.rem(tile + 1, TILES), lax.rem(tile + TILES - 1, TILES)
    members, height, wide = ens.shape
    columns = wide - 2 * BAND
    share = columns // LEV
    levels = height * LEV

    def lev_at(r):
        return lax.rem(lev + r, LEV)

    def group_at(r):
        return lax.rem(mine + r, GROUPS)

    def z_at(r):
        return lax.rem(z + r, Z)

    def tile_of(group, zz):
        return ((group // 2) * Z + zz) * 2 + lax.rem(group, 2)

    def rows(g):
        return pl.ds(pl.multiple_of(g * height, height), height)

    def lanes(g):
        return pl.ds(pl.multiple_of(g * share, share), share)

    def send(src, dst, send_sem, recv_sem, **target):
        pltpu.make_async_remote_copy(
            src_ref=src, dst_ref=dst, send_sem=send_sem, recv_sem=recv_sem,
            device_id=target, device_id_type=MESH,
        ).start()

    def signal(sem, **target):
        pl.semaphore_signal(sem, inc=1, device_id=target, device_id_type=MESH)

    def all_sent(ref, sem):
        pltpu.make_async_remote_copy(
            src_ref=ref, dst_ref=ref, send_sem=sem, recv_sem=sem,
            device_id={"tile": right}, device_id_type=MESH,
        ).wait_send()

    def all_here(ref, sem):
        pltpu.make_async_remote_copy(
            src_ref=ref, dst_ref=ref, send_sem=sem, recv_sem=sem,
            device_id={"tile": right}, device_id_type=MESH,
        ).wait_recv()

    barrier = pltpu.get_barrier_semaphore()
    targets = [{"tile": tile_of(group_at(r), z)} for r in range(1, GROUPS)]
    targets += [{"lev": lev_at(r)} for r in range(1, LEV)]
    for target in targets:
        signal(barrier, **target)

    @pl.when(z > 0)
    def _():
        signal(barrier, tile=tile - 2)

    @pl.when(z < Z - 1)
    def _():
        signal(barrier, tile=tile + 2)

    @pl.when(jnp.logical_and(core == 0, z > 0))
    def _():
        signal(barrier, tile=left)

    @pl.when(jnp.logical_and(core == 1, z < Z - 1))
    def _():
        signal(barrier, tile=right)

    lower, higher = (z + Z - 1) // Z, (2 * Z - 2 - z) // Z
    greeted = len(targets) + lower + higher + (1 - core) * lower + core * higher

    own = (
        pltpu.make_async_copy(ensemble, ens.at[:, :, pl.ds(BAND, columns)], local.at[0]),
        pltpu.make_async_copy(ensemble.at[:, :, lanes(lev)], other.at[:, rows(lev)], local.at[1]),
    )
    for copy in own:
        copy.start()

    row = lax.broadcasted_iota(jnp.int32, (GROUPS * 16, 768), 0)
    named = ((row >> 5) * Z + (row & 15)) * 2 + ((row >> 4) & 1)
    hit = jnp.logical_and(owner[...] == named, (row & 15) < Z)
    hits = bits(hit)
    upper = bits(
        lax.broadcasted_iota(jnp.int32, (256, 256), 0)
        < lax.broadcasted_iota(jnp.int32, (256, 256), 1)
    )
    base = jnp.zeros((GROUPS * 16, 1), jnp.float32)
    for b in range(3):
        part = slice(b * 256, b * 256 + 256)
        before = jnp.dot(hits[:, part], upper, preferred_element_type=jnp.float32) + base
        rank[:, part] = jnp.where(hit[:, part], before, -1.0)
        base = base + jnp.sum(hits[:, part].astype(jnp.float32), axis=1, keepdims=True)
    high, middle, low = split3(profile[...])
    col = column[...]
    which = lax.broadcasted_iota(jnp.int32, (16, 768), 0)
    cols = jnp.where(which == 0, col & -8, jnp.where(which == 1, col & 7, 0))
    table = jnp.concatenate(
        [high, middle, low, cols.astype(jnp.float32).astype(jnp.bfloat16)]
        + [jnp.zeros((64, 768), jnp.bfloat16)],
        axis=0,
    )
    lane = lax.broadcasted_iota(jnp.int32, (GROUPS * 16, 128), 1)
    spread = lax.broadcasted_iota(jnp.int32, (GROUPS * 16, 256), 1) - 16 * (
        lax.broadcasted_iota(jnp.int32, (GROUPS * 16, 256), 0) & 15
    )
    places = jnp.zeros((GROUPS * 16, 256), jnp.float32)
    for half in range(2):
        packed = jnp.zeros((GROUPS * 16, 128), jnp.float32)
        for s in range(half * 8, half * 8 + 8):
            got = lax.dot_general(
                bits(rank[...] == float(s)),
                table,
                (((1,), (1,)), ((), ())),
                preferred_element_type=jnp.float32,
            )
            value = got + pltpu.roll(got, 112, 1) + pltpu.roll(got, 96, 1)
            at = (s - half * 8) * 16
            value = pltpu.roll(value, at, 1) if at else value
            packed = jnp.where((lane >> 4) == (s - half * 8), value, packed)
            places = jnp.where(spread == s, got[:, 48:49] + got[:, 49:50], places)
        sorted_[:, half * 128 : half * 128 + 128] = packed
    for j in range(GROUPS):
        sorted_[j * 16 + Z : j * 16 + Z + 1, :] = jnp.sum(
            places[j * 16 : j * 16 + 16], axis=0, keepdims=True
        )

    pl.semaphore_wait(barrier, greeted)

    @pl.when(z > 0)
    def _():
        pl.semaphore_wait(up, 1)

    @pl.when(z < Z - 1)
    def _():
        signal(up, tile=tile + 2)

    def tell(r, carry):
        signal(ready, tile=tile - 2 * r)
        return carry

    lax.fori_loop(1, z + 1, tell, 0)

    for r in range(1, GROUPS):
        there = group_at(r)
        send(
            sorted_.at[pl.ds(pl.multiple_of(there * 16, 16), 16)], first.at[r], a_send, a_recv,
            tile=tile_of(there, z),
        )
    send(
        ensemble.at[:, :, pl.ds(columns - BAND, BAND)], ens.at[:, :, pl.ds(0, BAND)],
        eh_send, eh_recv.at[0], tile=right,
    )

    def to_left():
        send(
            ensemble.at[:, :, pl.ds(0, BAND)], ens.at[:, :, pl.ds(BAND + columns, BAND)],
            eh_send, eh_recv.at[1], tile=left,
        )

    def to_levels():
        for r in range(1, LEV):
            send(
                ensemble.at[:, :, lanes(lev_at(r))], other.at[:, rows(lev)], e_send, e_recv,
                lev=lev_at(r),
            )

    pl.when(2 * z + core > 0)(to_left)
    pl.when(z < EARLY)(to_levels)

    apart = (
        lax.broadcasted_iota(jnp.int32, hor.shape, 0)
        - lax.broadcasted_iota(jnp.int32, hor.shape, 1)
        - BAND
    )
    apart = jnp.abs(apart)
    hor[...] = jnp.where(
        apart <= BAND, jnp.exp(-apart.astype(jnp.float32) / BAND) / math.sqrt(BAND), 0.0
    ).astype(jnp.bfloat16)
    to, of = (lax.broadcasted_iota(jnp.int32, ver.shape, n) for n in range(2))
    apart = (to - of).astype(jnp.float32)
    ver[...] = jnp.where(
        (to // levels) == (of // levels),
        jnp.exp(-(apart * apart) / (2.0 * VSCALE * VSCALE)) / math.sqrt(VSCALE),
        0.0,
    ).astype(jnp.bfloat16)
    third[pl.ds(Z, 16 - Z)] = jnp.zeros((16 - Z, 8, 384), jnp.float32)

    first[0] = sorted_[pl.ds(pl.multiple_of(mine * 16, 16), 16)]
    all_here(first.at[pl.ds(1, GROUPS - 1)], a_recv)
    places = first[:, Z, :]
    for zz in range(Z):
        second[zz, :, 0:256] = first[:, zz, :]
        turned = pltpu.roll(places, 256 - 16 * zz, 1) if zz else places
        second[zz, :, 256:384] = turned[:, 0:128]
    def along_z(r, carry):
        send(second.at[z_at(r)], third.at[r], b_send, b_recv, tile=tile_of(mine, z_at(r)))
        return carry

    lax.fori_loop(Z - z, Z, along_z, 0)

    @pl.when(z < Z - 1)
    def _():
        pl.semaphore_wait(ready, Z - 1 - z)

    lax.fori_loop(1, Z - z, along_z, 0)
    third[0] = second[z]
    pl.when(2 * z + core == 0)(to_left)
    pl.when(z >= EARLY)(to_levels)
    all_here(third.at[pl.ds(1, Z - 1)], b_recv)

    where = third[:, :, 256:384].reshape(128, 128)
    cell = lax.broadcasted_iota(jnp.int32, (128, columns), 1).astype(jnp.float32)
    for half in range(2):
        turned = third[:, :, half * 128 : half * 128 + 128].reshape(128, 128).T
        pieces = split3(turned)
        for k in range(8):
            s = half * 8 + k
            for n, piece in enumerate(pieces):
                lhs[n * 16 : n * 16 + 16, s * 128 : s * 128 + 128] = piece[k * 16 : k * 16 + 16]
            hot[s * 128 : s * 128 + 128, :] = bits(where[:, s : s + 1] == cell)
    added = jnp.dot(lhs[...], hot[...], preferred_element_type=jnp.float32)
    added = added[0:16] + added[16:32] + added[32:48]
    field[:, pl.ds(BAND, columns)] = control[...] + added

    send(
        field.at[:, pl.ds(columns, BAND)], field.at[:, pl.ds(0, BAND)],
        fh_send, fh_recv.at[0], tile=right,
    )
    send(
        field.at[:, pl.ds(BAND, BAND)], field.at[:, pl.ds(BAND + columns, BAND)],
        fh_send, fh_recv.at[1], tile=left,
    )
    for copy in own:
        copy.wait()
    for side, at in enumerate((0, BAND + columns)):
        all_here(ens.at[:, :, pl.ds(at, BAND)], eh_recv.at[side])
        all_here(field.at[:, pl.ds(at, BAND)], fh_recv.at[side])

    for n, (m0, count) in enumerate(CHUNKS):
        for m in range(count):
            weighted[m * height : (m + 1) * height, :] = (
                ens[m0 + m].astype(jnp.float32) * field[...]
            ).astype(jnp.bfloat16)
        for k in range(columns // 256):
            piece = jnp.dot(
                weighted[0 : count * height, k * 256 : k * 256 + 256 + 2 * BAND], hor[...],
                preferred_element_type=jnp.float32,
            ).astype(jnp.bfloat16)
            for h in range(2):
                smooth[2 * k + h, m0 : m0 + count] = piece[:, h * 128 : h * 128 + 128].reshape(
                    count, height, share
                )
        for r in range(1, LEV):
            send(
                smooth.at[lev_at(r), pl.ds(m0, count)], gathered.at[pl.ds(m0, count), rows(lev)],
                s_send, s_recv.at[n], lev=lev_at(r),
            )
        gathered[pl.ds(m0, count), rows(lev)] = smooth[lev, pl.ds(m0, count)]

    all_here(smooth.at[pl.ds(1, LEV - 1)], e_recv)
    total[...] = jnp.zeros_like(total)
    for n, (m0, count) in enumerate(CHUNKS):
        all_here(smooth.at[pl.ds(1, LEV - 1), pl.ds(m0, count)], s_recv.at[n])
        now = total[...]
        for m in range(m0, m0 + count, 4):
            pairs = [gathered[m + i : m + i + 2].reshape(2 * levels, share) for i in (0, 2)]
            vertical = jnp.dot(
                ver[...], jnp.concatenate(pairs, axis=1), preferred_element_type=jnp.float32
            ).astype(jnp.bfloat16).astype(jnp.float32)
            for i in range(4):
                down, over = (i % 2) * levels, (i // 2) * share
                now += other[m + i].astype(jnp.float32) * vertical[
                    down : down + levels, over : over + share
                ]
        total[...] = now

    for r in range(1, LEV):
        send(total.at[rows(lev_at(r))], back.at[:, lanes(lev)], t_send, t_recv, lev=lev_at(r))
    back[:, lanes(lev)] = total[rows(lev)]
    all_here(total.at[pl.ds(0, levels - height)], t_recv)
    out[...] = back[...] * (1.0 / (members - 1))

    all_sent(first.at[pl.ds(1, GROUPS - 1)], a_send)
    all_sent(third.at[pl.ds(1, Z - 1)], b_send)
    all_sent(smooth.at[pl.ds(1, LEV - 1)], e_send)
    all_sent(ens.at[:, :, pl.ds(BAND, columns)], eh_send)
    all_sent(field.at[:, pl.ds(BAND, columns)], fh_send)
    all_sent(smooth.at[pl.ds(1, LEV - 1)], s_send)
    all_sent(total.at[pl.ds(0, levels - height)], t_send)


def shards(control, ensemble, obs_owner, obs_column, obs_profile):
    members, height, columns = ensemble.shape
    levels, wide, share = height * LEV, columns + 2 * BAND, columns // LEV
    vmem = pl.BlockSpec(memory_space=pltpu.VMEM)
    dma = pltpu.SemaphoreType.DMA
    f32, bf16 = jnp.float32, jnp.bfloat16
    return pl.pallas_call(
        kernel,
        out_shape=jax.ShapeDtypeStruct(control.shape, f32),
        in_specs=[vmem, pl.BlockSpec(memory_space=pl.ANY), vmem, vmem, vmem],
        out_specs=vmem,
        scratch_shapes=[
            pltpu.VMEM((members, height, wide), bf16),
            pltpu.VMEM((height, wide), f32),
            pltpu.VMEM((max(n for _, n in CHUNKS) * height, wide), bf16),
            pltpu.VMEM((256 + 2 * BAND, 256), bf16),
            pltpu.VMEM((2 * levels, 2 * levels), bf16),
            pltpu.VMEM((GROUPS * 16, 768), f32),
            pltpu.VMEM((GROUPS * 16, 256), f32),
            pltpu.VMEM((GROUPS, 16, 256), f32),
            pltpu.VMEM((Z, 8, 384), f32),
            pltpu.VMEM((16, 8, 384), f32),
            pltpu.VMEM((48, SLOTS * 128), bf16),
            pltpu.VMEM((SLOTS * 128, columns), bf16),
            pltpu.VMEM((LEV, members, height, share), bf16),
            pltpu.VMEM((members, levels, share), bf16),
            pltpu.VMEM((members, levels, share), bf16),
            pltpu.VMEM((levels, share), f32),
            pltpu.VMEM((height, columns), f32),
            dma((2,)), dma, dma, dma, dma, dma, dma, dma, dma((2,)),
            dma, dma((2,)), dma, dma((len(CHUNKS),)), dma, dma,
            pltpu.SemaphoreType.REGULAR, pltpu.SemaphoreType.REGULAR,
        ],
        compiler_params=pltpu.CompilerParams(
            collective_id=0, has_side_effects=True, vmem_limit_bytes=60 << 20
        ),
    )(control, ensemble, obs_owner.reshape(1, -1), obs_column.reshape(1, -1), obs_profile)


def solution(mesh):
    in_specs = (
        P("lev", "tile"),
        P(None, "lev", "tile"),
        P("tile", None),
        P("tile"),
        P("lev", "tile"),
    )
    out_specs = P("lev", "tile")
    return jax.shard_map(shards, mesh=mesh, in_specs=in_specs, out_specs=out_specs, check_vma=False)
```

time: 157 us -> 62.6 us (0.40)
  the two profiles are of different devices: /device:TPU:8 before, /device:TPU:1 now
where the time goes in v2:
time: 62.6 us; the launch traced here: 62.4 us
  Pallas kernels  59.6 us (95%)
  local copies, waits for them, and re-layouts  2.74 us (4%)
    pallas_call x1, Pallas kernels, shards(): pl.pallas_call(kernel, out_shape=jax.ShapeDtypeStruct(control.shape, f32)...  59.6 us
    unnamed x1, local copies, waits for them, and re-layouts  1.47 us
    reshape x1, local copies, waits for them, and re-layouts, shards(): obs_column.reshape(1, -1)  1.27 us

profile of v2, /device:TPU:1, one launch (start us, length us, event | category | flops | bytes accessed | tf_op | source)
XLA Modules:
  0.0 62.4 jit_solution(2514982295624688330)
XLA Ops:
  0.0 1.3 %reshape.7.column = s32[1,768]{1,0:T(1,128)} reshape(s32[768]{0:T(1024)} %param.8) | data formatting | bytes 6144 | tf_op jit(solution)/shard_map/reshape | solution.py:371
  1.3 59.6 %shard_map.55 = f32[16,1024]{1,0:T(8,128)} custom-call(f32[16,1024]{1,0:T(8,128)} %control.1, bf16[32,16,1024]{2,1,0:T(8,128)(2,1)} %ensemble.1, s32[1,768]{1,0:T(1,128)} %bitcast.1, s32[1,768]{1,0:T(1,128)} %reshape.7.column, f32[16,768]{1,0:T(8,128)} %profile.1), custom_call_target="tpu_custom_call" | custom-call | tf_op jit(solution)/shard_map/pallas_call | solution.py:341
  60.9 1.5 %copy.7 = f32[16,1024]{1,0:T(8,128)} copy(f32[16,1024]{1,0:T(8,128)} %shard_map.55) | data formatting | bytes 131072

commit v3 on v2

--- a/solution.py
+++ b/solution.py
@@ -16,7 +16,7 @@
 GROUPS = 2 * Y_HI
 SLOTS = 16
 BAND = 512
-EARLY = 9
+EARLY = 11
 CHUNKS = ((0, 8), (8, 8), (16, 8), (24, 8))
 
 
@@ -33,9 +33,9 @@
 
 
 def kernel(
-    control, ensemble, owner, column, profile, out,
+    control_in, ensemble, owner_in, column_in, profile_in, out,
     ens, field, weighted, hor, ver, rank, sorted_, first, second, third, lhs, hot,
-    smooth, gathered, other, total, back,
+    smooth, gathered, other, total, control, owner, column, profile,
     local, a_send, a_recv, b_send, b_recv, e_send, e_recv, eh_send, eh_recv,
     fh_send, fh_recv, s_send, s_recv, t_send, t_recv, up, ready,
 ):
@@ -112,12 +112,23 @@
     lower, higher = (z + Z - 1) // Z, (2 * Z - 2 - z) // Z
     greeted = len(targets) + lower + higher + (1 - core) * lower + core * higher
 
+    first_needed = [
+        pltpu.make_async_copy(src, dst, local.at[2 + n])
+        for n, (src, dst) in enumerate(
+            ((owner_in, owner), (column_in, column), (profile_in, profile))
+        )
+    ]
     own = (
         pltpu.make_async_copy(ensemble, ens.at[:, :, pl.ds(BAND, columns)], local.at[0]),
         pltpu.make_async_copy(ensemble.at[:, :, lanes(lev)], other.at[:, rows(lev)], local.at[1]),
-    )
+        pltpu.make_async_copy(control_in, control, local.at[5]),
+    )
+    for copy in first_needed:
+        copy.start()
     for copy in own:
         copy.start()
+    for copy in first_needed:
+        copy.wait()
 
     row = lax.broadcasted_iota(jnp.int32, (GROUPS * 16, 768), 0)
     named = ((row >> 5) * Z + (row & 15)) * 2 + ((row >> 4) & 1)
@@ -134,7 +145,7 @@
         rank[:, part] = jnp.where(hit[:, part], before, -1.0)
         base = base + jnp.sum(hits[:, part].astype(jnp.float32), axis=1, keepdims=True)
     high, middle, low = split3(profile[...])
-    col = column[...]
+    col = column[...].reshape(1, -1)
     which = lax.broadcasted_iota(jnp.int32, (16, 768), 0)
     cols = jnp.where(which == 0, col & -8, jnp.where(which == 1, col & 7, 0))
     table = jnp.concatenate(
@@ -236,7 +247,7 @@
         turned = pltpu.roll(places, 256 - 16 * zz, 1) if zz else places
         second[zz, :, 256:384] = turned[:, 0:128]
     def along_z(r, carry):
-        send(second.at[z_at(r)], third.at[r], b_send, b_recv, tile=tile_of(mine, z_at(r)))
+        send(second.at[z_at(r)], third.at[z], b_send, b_recv.at[z], tile=tile_of(mine, z_at(r)))
         return carry
 
     lax.fori_loop(Z - z, Z, along_z, 0)
@@ -246,24 +257,42 @@
         pl.semaphore_wait(ready, Z - 1 - z)
 
     lax.fori_loop(1, Z - z, along_z, 0)
-    third[0] = second[z]
+    third[z] = second[z]
     pl.when(2 * z + core == 0)(to_left)
     pl.when(z >= EARLY)(to_levels)
-    all_here(third.at[pl.ds(1, Z - 1)], b_recv)
-
-    where = third[:, :, 256:384].reshape(128, 128)
-    cell = lax.broadcasted_iota(jnp.int32, (128, columns), 1).astype(jnp.float32)
-    for half in range(2):
-        turned = third[:, :, half * 128 : half * 128 + 128].reshape(128, 128).T
-        pieces = split3(turned)
-        for k in range(8):
-            s = half * 8 + k
-            for n, piece in enumerate(pieces):
-                lhs[n * 16 : n * 16 + 16, s * 128 : s * 128 + 128] = piece[k * 16 : k * 16 + 16]
-            hot[s * 128 : s * 128 + 128, :] = bits(where[:, s : s + 1] == cell)
-    added = jnp.dot(lhs[...], hot[...], preferred_element_type=jnp.float32)
-    added = added[0:16] + added[16:32] + added[32:48]
-    field[:, pl.ds(BAND, columns)] = control[...] + added
+
+    cell = lax.broadcasted_iota(jnp.int32, (64, columns), 1).astype(jnp.float32)
+
+    def arrived(n):
+        @pl.when(z != n)
+        def _():
+            all_here(third.at[n], b_recv.at[n])
+
+    def scattered(start):
+        where = third[start : start + 8, :, 256:384].reshape(64, 128)
+        for half in range(2):
+            block = third[start : start + 8, :, half * 128 : half * 128 + 128].reshape(64, 128)
+            turned = jnp.concatenate([block, pltpu.roll(block, 112, 1)], axis=0).T
+            pieces = split3(turned)
+            for k in range(4):
+                pair = half * 4 + k
+                part = slice(pair * 128, pair * 128 + 128)
+                for n, piece in enumerate(pieces):
+                    lhs[n * 16 : n * 16 + 16, part] = piece[k * 32 : k * 32 + 16]
+                for i in range(2):
+                    s = 2 * pair + i
+                    hot[s * 64 : s * 64 + 64, :] = bits(where[:, s : s + 1] == cell)
+        added = jnp.dot(lhs[...], hot[...], preferred_element_type=jnp.float32)
+        return added[0:16] + added[16:32] + added[32:48]
+
+    for copy in own:
+        copy.wait()
+    for n in range(8):
+        arrived(n)
+    field[:, pl.ds(BAND, columns)] = control[...] + scattered(0)
+    for n in range(8, Z):
+        arrived(n)
+    field[:, pl.ds(BAND, columns)] += scattered(8)
 
     send(
         field.at[:, pl.ds(columns, BAND)], field.at[:, pl.ds(0, BAND)],
@@ -273,8 +302,6 @@
         field.at[:, pl.ds(BAND, BAND)], field.at[:, pl.ds(BAND + columns, BAND)],
         fh_send, fh_recv.at[1], tile=left,
     )
-    for copy in own:
-        copy.wait()
     for side, at in enumerate((0, BAND + columns)):
         all_here(ens.at[:, :, pl.ds(at, BAND)], eh_recv.at[side])
         all_here(field.at[:, pl.ds(at, BAND)], fh_recv.at[side])
@@ -318,10 +345,11 @@
         total[...] = now
 
     for r in range(1, LEV):
-        send(total.at[rows(lev_at(r))], back.at[:, lanes(lev)], t_send, t_recv, lev=lev_at(r))
-    back[:, lanes(lev)] = total[rows(lev)]
+        send(total.at[rows(lev_at(r))], out.at[:, lanes(lev)], t_send, t_recv, lev=lev_at(r))
+    kept = pltpu.make_async_copy(total.at[rows(lev)], out.at[:, lanes(lev)], local.at[6])
+    kept.start()
+    kept.wait()
     all_here(total.at[pl.ds(0, levels - height)], t_recv)
-    out[...] = back[...] * (1.0 / (members - 1))
 
     all_sent(first.at[pl.ds(1, GROUPS - 1)], a_send)
     all_sent(third.at[pl.ds(1, Z - 1)], b_send)
@@ -335,14 +363,13 @@
 def shards(control, ensemble, obs_owner, obs_column, obs_profile):
     members, height, columns = ensemble.shape
     levels, wide, share = height * LEV, columns + 2 * BAND, columns // LEV
-    vmem = pl.BlockSpec(memory_space=pltpu.VMEM)
     dma = pltpu.SemaphoreType.DMA
     f32, bf16 = jnp.float32, jnp.bfloat16
-    return pl.pallas_call(
+    sums = pl.pallas_call(
         kernel,
         out_shape=jax.ShapeDtypeStruct(control.shape, f32),
-        in_specs=[vmem, pl.BlockSpec(memory_space=pl.ANY), vmem, vmem, vmem],
-        out_specs=vmem,
+        in_specs=[pl.BlockSpec(memory_space=pl.ANY)] * 5,
+        out_specs=pl.BlockSpec(memory_space=pl.ANY),
         scratch_shapes=[
             pltpu.VMEM((members, height, wide), bf16),
             pltpu.VMEM((height, wide), f32),
@@ -354,21 +381,25 @@
             pltpu.VMEM((GROUPS, 16, 256), f32),
             pltpu.VMEM((Z, 8, 384), f32),
             pltpu.VMEM((16, 8, 384), f32),
-            pltpu.VMEM((48, SLOTS * 128), bf16),
-            pltpu.VMEM((SLOTS * 128, columns), bf16),
+            pltpu.VMEM((48, SLOTS * 64), bf16),
+            pltpu.VMEM((SLOTS * 64, columns), bf16),
             pltpu.VMEM((LEV, members, height, share), bf16),
             pltpu.VMEM((members, levels, share), bf16),
             pltpu.VMEM((members, levels, share), bf16),
             pltpu.VMEM((levels, share), f32),
             pltpu.VMEM((height, columns), f32),
-            dma((2,)), dma, dma, dma, dma, dma, dma, dma, dma((2,)),
+            pltpu.VMEM((1,) + obs_column.shape, jnp.int32),
+            pltpu.VMEM(obs_column.shape, jnp.int32),
+            pltpu.VMEM(obs_profile.shape, f32),
+            dma((7,)), dma, dma, dma, dma((Z,)), dma, dma, dma, dma((2,)),
             dma, dma((2,)), dma, dma((len(CHUNKS),)), dma, dma,
             pltpu.SemaphoreType.REGULAR, pltpu.SemaphoreType.REGULAR,
         ],
         compiler_params=pltpu.CompilerParams(
             collective_id=0, has_side_effects=True, vmem_limit_bytes=60 << 20
         ),
-    )(control, ensemble, obs_owner.reshape(1, -1), obs_column.reshape(1, -1), obs_profile)
+    )(control, ensemble, obs_owner.reshape(1, -1), obs_column, obs_profile)
+    return sums * (1.0 / (members - 1))
 
 
 def solution(mesh):

time: 62.6 us -> 59.9 us (0.957)
  local copies, waits for them, and re-layouts: 2.74 us -> 0 us
  other arithmetic: 0 us -> 1.48 us
  Pallas kernels: 59.6 us -> 58.2 us
    mul x0 -> x1, other arithmetic: none -> 1.48 us  [shards(): return sums * (1.0 / (members - 1))]
    unnamed x1 -> x0, local copies, waits for them, and re-layouts: 1.47 us -> none
    pallas_call x1, Pallas kernels: 59.6 us -> 58.2 us  [shards(): pl.pallas_call(kernel, out_shape=jax.ShapeDtypeStruct(control.shape, f32)...]
    reshape x1 -> x0, local copies, waits for them, and re-layouts: 1.27 us -> none  [shards(): obs_column.reshape(1, -1)]
where the time goes in v3:
time: 59.9 us; the launch traced here: 59.7 us
  Pallas kernels  58.2 us (97%)
  other arithmetic  1.48 us (2%)
    pallas_call x1, Pallas kernels, shards(): pl.pallas_call(kernel, out_shape=jax.ShapeDtypeStruct(control.shape, f32)...  58.2 us
    mul x1, other arithmetic, shards(): return sums * (1.0 / (members - 1))  1.48 us

profile of v3, /device:TPU:1, one launch (start us, length us, event | category | flops | bytes accessed | tf_op | source)
XLA Modules:
  0.0 59.7 jit_solution(4915421736074585526)
XLA Ops:
  0.0 58.2 %shard_map.55 = f32[16,1024]{1,0:T(8,128)} custom-call(f32[16,1024]{1,0:T(8,128)} %control_in.1, bf16[32,16,1024]{2,1,0:T(8,128)(2,1)} %ensemble.1, s32[1,768]{1,0:T(1,128)} %bitcast.1, s32[768]{0:T(1024)} %column_in.1, f32[16,768]{1,0:T(8,128)} %profile_in.1), custom_call_target="tpu_custom_call" | custom-call | tf_op jit(solution)/shard_map/pallas_call | solution.py:368
  58.2 1.5 %broadcast_multiply_fusion = f32[16,1024]{1,0:T(8,128)} fusion(f32[16,1024]{1,0:T(8,128)} %shard_map.55), kind=kLoop, calls=%fused_computation | loop fusion | flops 16384 | bytes 131072 | tf_op jit(solution)/shard_map/mul | solution.py:402

commit v4 on v3

--- a/solution.py
+++ b/solution.py
@@ -17,7 +17,8 @@
 SLOTS = 16
 BAND = 512
 EARLY = 11
-CHUNKS = ((0, 8), (8, 8), (16, 8), (24, 8))
+FAR_FIRST = (4, 5, 3, 6, 2, 7, 1)
+CHUNKS = ((0, 4), (4, 8), (12, 8), (20, 8), (28, 4))
 
 
 def split3(x):
@@ -37,7 +38,7 @@
     ens, field, weighted, hor, ver, rank, sorted_, first, second, third, lhs, hot,
     smooth, gathered, other, total, control, owner, column, profile,
     local, a_send, a_recv, b_send, b_recv, e_send, e_recv, eh_send, eh_recv,
-    fh_send, fh_recv, s_send, s_recv, t_send, t_recv, up, ready,
+    fh_send, fh_recv, s_send, s_recv, t_send, t_recv, up, ready, around,
 ):
     tile, lev = lax.axis_index("tile"), lax.axis_index("lev")
     core, z, y_hi = lax.rem(tile, 2), lax.rem(tile // 2, Z), tile // (2 * Z)
@@ -88,8 +89,8 @@
         ).wait_recv()
 
     barrier = pltpu.get_barrier_semaphore()
-    targets = [{"tile": tile_of(group_at(r), z)} for r in range(1, GROUPS)]
-    targets += [{"lev": lev_at(r)} for r in range(1, LEV)]
+    targets = [{"tile": tile_of(group_at(r), z)} for r in FAR_FIRST]
+    targets += [{"lev": lev_at(r)} for r in FAR_FIRST]
     for target in targets:
         signal(barrier, **target)
 
@@ -180,26 +181,31 @@
 
     pl.semaphore_wait(barrier, greeted)
 
-    @pl.when(z > 0)
-    def _():
-        pl.semaphore_wait(up, 1)
-
-    @pl.when(z < Z - 1)
-    def _():
-        signal(up, tile=tile + 2)
-
-    def tell(r, carry):
-        signal(ready, tile=tile - 2 * r)
-        return carry
-
-    lax.fori_loop(1, z + 1, tell, 0)
-
-    for r in range(1, GROUPS):
+    for r in FAR_FIRST:
         there = group_at(r)
         send(
             sorted_.at[pl.ds(pl.multiple_of(there * 16, 16), 16)], first.at[r], a_send, a_recv,
             tile=tile_of(there, z),
         )
+
+    @pl.when(z > 0)
+    def _():
+        pl.semaphore_wait(up, 1)
+
+    @pl.when(z < Z - 1)
+    def _():
+        signal(up, tile=tile + 2)
+
+    def tell(r, carry):
+        signal(ready, tile=tile - 2 * r)
+        return carry
+
+    lax.fori_loop(1, 1 + z * higher, tell, 0)
+
+    @pl.when(z == Z - 1)
+    def _():
+        signal(around, tile=tile - 2 * (Z - 1))
+
     send(
         ensemble.at[:, :, pl.ds(columns - BAND, BAND)], ens.at[:, :, pl.ds(0, BAND)],
         eh_send, eh_recv.at[0], tile=right,
@@ -212,7 +218,7 @@
         )
 
     def to_levels():
-        for r in range(1, LEV):
+        for r in FAR_FIRST:
             send(
                 ensemble.at[:, :, lanes(lev_at(r))], other.at[:, rows(lev)], e_send, e_recv,
                 lev=lev_at(r),
@@ -252,12 +258,17 @@
 
     lax.fori_loop(Z - z, Z, along_z, 0)
 
-    @pl.when(z < Z - 1)
-    def _():
-        pl.semaphore_wait(ready, Z - 1 - z)
+    @pl.when(z < Z - 2)
+    def _():
+        pl.semaphore_wait(ready, Z - 2 - z)
 
     lax.fori_loop(1, Z - z, along_z, 0)
     third[z] = second[z]
+
+    @pl.when(z == 0)
+    def _():
+        pl.semaphore_wait(around, 1)
+
     pl.when(2 * z + core == 0)(to_left)
     pl.when(z >= EARLY)(to_levels)
 
@@ -320,7 +331,7 @@
                 smooth[2 * k + h, m0 : m0 + count] = piece[:, h * 128 : h * 128 + 128].reshape(
                     count, height, share
                 )
-        for r in range(1, LEV):
+        for r in FAR_FIRST:
             send(
                 smooth.at[lev_at(r), pl.ds(m0, count)], gathered.at[pl.ds(m0, count), rows(lev)],
                 s_send, s_recv.at[n], lev=lev_at(r),
@@ -344,7 +355,7 @@
                 ]
         total[...] = now
 
-    for r in range(1, LEV):
+    for r in FAR_FIRST:
         send(total.at[rows(lev_at(r))], out.at[:, lanes(lev)], t_send, t_recv, lev=lev_at(r))
     kept = pltpu.make_async_copy(total.at[rows(lev)], out.at[:, lanes(lev)], local.at[6])
     kept.start()
@@ -393,7 +404,7 @@
             pltpu.VMEM(obs_profile.shape, f32),
             dma((7,)), dma, dma, dma, dma((Z,)), dma, dma, dma, dma((2,)),
             dma, dma((2,)), dma, dma((len(CHUNKS),)), dma, dma,
-            pltpu.SemaphoreType.REGULAR, pltpu.SemaphoreType.REGULAR,
+            pltpu.SemaphoreType.REGULAR, pltpu.SemaphoreType.REGULAR, pltpu.SemaphoreType.REGULAR,
         ],
         compiler_params=pltpu.CompilerParams(
             collective_id=0, has_side_effects=True, vmem_limit_bytes=60 << 20

time: 59.9 us -> 60.1 us (level)
  no operation moved by 1% of the time
where the time goes in v4:
time: 60.1 us; the launch traced here: 59.9 us
  Pallas kernels  58.4 us (97%)
  other arithmetic  1.48 us (2%)
    pallas_call x1, Pallas kernels, shards(): pl.pallas_call(kernel, out_shape=jax.ShapeDtypeStruct(control.shape, f32)...  58.4 us
    mul x1, other arithmetic, shards(): return sums * (1.0 / (members - 1))  1.48 us

profile of v4, /device:TPU:1, one launch (start us, length us, event | category | flops | bytes accessed | tf_op | source)
XLA Modules:
  0.0 59.9 jit_solution(3392623324967367824)
XLA Ops:
  0.0 58.4 %shard_map.55 = f32[16,1024]{1,0:T(8,128)} custom-call(f32[16,1024]{1,0:T(8,128)} %control_in.1, bf16[32,16,1024]{2,1,0:T(8,128)(2,1)} %ensemble.1, s32[1,768]{1,0:T(1,128)} %bitcast.1, s32[768]{0:T(1024)} %column_in.1, f32[16,768]{1,0:T(8,128)} %profile_in.1), custom_call_target="tpu_custom_call" | custom-call | tf_op jit(solution)/shard_map/pallas_call | solution.py:379
  58.4 1.5 %broadcast_multiply_fusion = f32[16,1024]{1,0:T(8,128)} fusion(f32[16,1024]{1,0:T(8,128)} %shard_map.55), kind=kLoop, calls=%fused_computation | loop fusion | flops 16384 | bytes 131072 | tf_op jit(solution)/shard_map/mul | solution.py:413

commit v5 on v4

--- a/solution.py
+++ b/solution.py
@@ -313,18 +313,27 @@
         field.at[:, pl.ds(BAND, BAND)], field.at[:, pl.ds(BAND + columns, BAND)],
         fh_send, fh_recv.at[1], tile=left,
     )
+    def weigh(m0, count, at, width):
+        here = field[:, at : at + width]
+        for m in range(m0, m0 + count):
+            weighted[m * height : (m + 1) * height, at : at + width] = (
+                ens[m, :, at : at + width].astype(jnp.float32) * here
+            ).astype(jnp.bfloat16)
+
+    weigh(0, members, BAND, columns)
     for side, at in enumerate((0, BAND + columns)):
         all_here(ens.at[:, :, pl.ds(at, BAND)], eh_recv.at[side])
         all_here(field.at[:, pl.ds(at, BAND)], fh_recv.at[side])
 
     for n, (m0, count) in enumerate(CHUNKS):
-        for m in range(count):
-            weighted[m * height : (m + 1) * height, :] = (
-                ens[m0 + m].astype(jnp.float32) * field[...]
-            ).astype(jnp.bfloat16)
+        for at in (0, BAND + columns):
+            weigh(m0, count, at, BAND)
         for k in range(columns // 256):
             piece = jnp.dot(
-                weighted[0 : count * height, k * 256 : k * 256 + 256 + 2 * BAND], hor[...],
+                weighted[
+                    m0 * height : (m0 + count) * height, k * 256 : k * 256 + 256 + 2 * BAND
+                ],
+                hor[...],
                 preferred_element_type=jnp.float32,
             ).astype(jnp.bfloat16)
             for h in range(2):
@@ -384,7 +393,7 @@
         scratch_shapes=[
             pltpu.VMEM((members, height, wide), bf16),
             pltpu.VMEM((height, wide), f32),
-            pltpu.VMEM((max(n for _, n in CHUNKS) * height, wide), bf16),
+            pltpu.VMEM((members * height, wide), bf16),
             pltpu.VMEM((256 + 2 * BAND, 256), bf16),
             pltpu.VMEM((2 * levels, 2 * levels), bf16),
             pltpu.VMEM((GROUPS * 16, 768), f32),

time: 60.1 us -> 60.1 us (level)
  no operation moved by 1% of the time
where the time goes in v5:
time: 60.1 us; the launch traced here: 59.9 us
  Pallas kernels  58.4 us (97%)
  other arithmetic  1.48 us (2%)
    pallas_call x1, Pallas kernels, shards(): pl.pallas_call(kernel, out_shape=jax.ShapeDtypeStruct(control.shape, f32)...  58.4 us
    mul x1, other arithmetic, shards(): return sums * (1.0 / (members - 1))  1.48 us

profile of v5, /device:TPU:1, one launch (start us, length us, event | category | flops | bytes accessed | tf_op | source)
XLA Modules:
  0.0 59.9 jit_solution(846275397751100814)
XLA Ops:
  0.0 58.4 %shard_map.55 = f32[16,1024]{1,0:T(8,128)} custom-call(f32[16,1024]{1,0:T(8,128)} %control_in.1, bf16[32,16,1024]{2,1,0:T(8,128)(2,1)} %ensemble.1, s32[1,768]{1,0:T(1,128)} %bitcast.1, s32[768]{0:T(1024)} %column_in.1, f32[16,768]{1,0:T(8,128)} %profile_in.1), custom_call_target="tpu_custom_call" | custom-call | tf_op jit(solution)/shard_map/pallas_call | solution.py:388
  58.4 1.5 %broadcast_multiply_fusion = f32[16,1024]{1,0:T(8,128)} fusion(f32[16,1024]{1,0:T(8,128)} %shard_map.55), kind=kLoop, calls=%fused_computation | loop fusion | flops 16384 | bytes 131072 | tf_op jit(solution)/shard_map/mul | solution.py:422
